TPU v7x, 32 devices: a whole 2x2x4 slice. The times are simulated.
32 devices in a mesh: dp: 2 (over core), fsdp: 16 (over z, y, x).
Axes of the slice: x: 2, y: 2, z: 4, core: 2. Of those that a mesh axis runs over, the one named last changes fastest.
Arguments:
- tokens: bfloat16 [8192, 1088], P(('dp', 'fsdp')), may hold values from -6 to 6
- cotangent: bfloat16 [8192, 1088], P(('dp', 'fsdp')), may hold values from -6 to 6
- lengths: int32 [32, 4], P(('dp', 'fsdp')), may hold values from 0 to 256, as said below
- triple_weight: float32 [1088, 3264], P('fsdp'), may hold values from -0.21875 to 0.21875
- triple_momentum: float32 [1088, 3264], P('fsdp'), may hold values from -32 to 32
- triple_variance: float32 [1088, 3264], P('fsdp'), may hold values from 155.648 to 622.592
- merge_weight: float32 [1088, 1088], P('fsdp'), may hold values from -0.75 to 0.75
- merge_momentum: float32 [1088, 1088], P('fsdp'), may hold values from -6 to 6
- merge_variance: float32 [1088, 1088], P('fsdp'), may hold values from 17.2032 to 68.8128
- expand_weight: float32 [1088, 4352], P('fsdp'), may hold values from -0.1875 to 0.1875
- expand_momentum: float32 [1088, 4352], P('fsdp'), may hold values from -16 to 16
- expand_variance: float32 [1088, 4352], P('fsdp'), may hold values from 29.4912 to 116.3264
- shrink_weight: float32 [4352, 1088], P('fsdp'), may hold values from -0.09375 to 0.09375
- shrink_momentum: float32 [4352, 1088], P('fsdp'), may hold values from -32 to 32
- shrink_variance: float32 [4352, 1088], P('fsdp'), may hold values from 130.2528 to 521.0112
- vector_weight: float32 [12, 1088], P(None, 'fsdp'), may hold values from -1.2 to 1.4
- vector_momentum: float32 [12, 1088], P(None, 'fsdp'), may hold values from -32 to 32
- vector_variance: float32 [12, 1088], P(None, 'fsdp'), may hold values from 106.496 to 434.176
Outputs:
- layer_output: bfloat16 [8192, 1088], P(('dp', 'fsdp'))
- input_grad: bfloat16 [8192, 1088], P(('dp', 'fsdp'))
- triple_next: float32 [1088, 3264], P('fsdp')
- momentum_triple: float32 [1088, 3264], P('fsdp')
- variance_triple: float32 [1088, 3264], P('fsdp')
- merge_next: float32 [1088, 1088], P('fsdp')
- momentum_merge: float32 [1088, 1088], P('fsdp')
- variance_merge: float32 [1088, 1088], P('fsdp')
- expand_next: float32 [1088, 4352], P('fsdp')
- momentum_expand: float32 [1088, 4352], P('fsdp')
- variance_expand: float32 [1088, 4352], P('fsdp')
- shrink_next: float32 [4352, 1088], P('fsdp')
- momentum_shrink: float32 [4352, 1088], P('fsdp')
- variance_shrink: float32 [4352, 1088], P('fsdp')
- vector_next: float32 [12, 1088], P(None, 'fsdp')
- momentum_vector: float32 [12, 1088], P(None, 'fsdp')
- variance_vector: float32 [12, 1088], P(None, 'fsdp')
Inputs may be any that keep to these rules, and one draw needn't show every extreme that they name: `lengths`: each row lists the sequences packed into one device's 256 slots from the start; the slots after their sum are padding. The first device holds one sequence of 256 tokens.
All inputs are finite; a program needn't handle non-finite values.
Results may differ from a plain program's by a relative error of at most 0.013.
The roundings to bfloat16 on the way count: a program that leaves them out, or rounds other values in their place, can miss the bound.
Values may be sent and summed in bfloat16 or wider, within the bound.
A program may use at most 192 MiB of HBM per device.

v0:
```python
import jax
import jax.numpy as jnp
from jax import lax
from jax.sharding import PartitionSpec as P

HEADS = 17
HEAD_DIM = 64
STEP = 10


norm_eps = 1e-05
beta_one = 0.9
beta_two = 0.95
adam_eps = 1e-08
rate_matrix = 0.05
rate_vector = 0.4
decay_matrix = 0.1
masked_score = -1e30


def layer_norm(values, gain_row, shift_row):
    center = values - jnp.mean(values, axis=-1, keepdims=True)
    spread = jnp.mean(center * center, axis=-1, keepdims=True)
    return center * lax.rsqrt(spread + norm_eps) * gain_row + shift_row


def gelu_tanh(values):
    return jax.nn.gelu(values, approximate=True)


def segments_of(length_row, total_rows):
    places = jnp.arange(total_rows, dtype=jnp.int32)
    bounds = jnp.cumsum(length_row)
    segment = jnp.sum((places[:, None] >= bounds[None, :]).astype(jnp.int32), axis=1)
    live_rows = (places < bounds[-1]).astype(jnp.float32)
    return (segment, live_rows)


def inner_rows(left_side, right_side):
    return lax.dot_general(
        left_side, right_side, (((0,), (0,)), ((), ())), preferred_element_type=jnp.float32
    )


def times_transposed(left_side, right_side):
    return lax.dot_general(
        left_side, right_side, (((1,), (1,)), ((), ())), preferred_element_type=jnp.float32
    )


def block_scores(queries, keys_low, segment, first_row, block_rows):
    total_rows = keys_low.shape[0]
    row_index = first_row + jnp.arange(block_rows, dtype=jnp.int32)
    column_index = jnp.arange(total_rows, dtype=jnp.int32)
    allowed = (segment[:, None] == segment[None, :]) & (column_index[None, :] <= row_index[:, None])
    scaling = queries.shape[-1] ** (-0.5)
    scores = (
        jnp.einsum("qhe,khe->hqk", queries, keys_low, preferred_element_type=jnp.float32) * scaling
    )
    return (jnp.where(allowed[None], scores, masked_score), queries)


def attend_forward(queries, keys_low, values_low, segment):
    total_rows = queries.shape[0]
    block_rows = min(512, total_rows)

    def forward_block(block_index):
        first_row = block_index * block_rows
        scores, query_part = block_scores(queries, keys_low, segment, first_row, block_rows)
        highest_score = jnp.max(scores, axis=-1, keepdims=True)
        weights = jnp.exp(scores - highest_score)
        totals = jnp.sum(weights, axis=-1, keepdims=True)
        probs_low = (weights / totals).astype(jnp.bfloat16)
        context = jnp.einsum(
            "hqk,khe->qhe", probs_low, values_low, preferred_element_type=jnp.float32
        )
        return (context, highest_score[..., 0] + jnp.log(totals[..., 0]))

    contexts, logsums = lax.map(
        forward_block, jnp.arange(total_rows // block_rows, dtype=jnp.int32)
    )
    return (contexts.reshape(queries.shape), logsums)


def attend_backward(queries, keys_low, values_low, logsums, grad_context, segment):
    total_rows = queries.shape[0]
    block_rows = min(512, total_rows)
    scaling = queries.shape[-1] ** (-0.5)

    def backward_block(running, inputs):
        grad_keys, grad_values = running
        block_index, logsum_block = inputs
        first_row = block_index * block_rows
        scores, query_part = block_scores(queries, keys_low, segment, first_row, block_rows)
        probability = jnp.exp(scores - logsum_block[..., None])
        probs_low = probability.astype(jnp.bfloat16)
        grad_probs = jnp.einsum(
            "qhe,khe->hqk", grad_context, values_low, preferred_element_type=jnp.float32
        )
        centered = grad_probs - jnp.sum(grad_probs * probability, axis=-1, keepdims=True)
        grad_scores = (probability * centered).astype(jnp.bfloat16)
        grad_query = (
            jnp.einsum("hqk,khe->qhe", grad_scores, keys_low, preferred_element_type=jnp.float32)
            * scaling
        )
        grad_keys = (
            grad_keys
            + jnp.einsum(
                "hqk,qhe->khe", grad_scores, query_part, preferred_element_type=jnp.float32
            )
            * scaling
        )
        grad_values = grad_values + jnp.einsum(
            "hqk,qhe->khe", probs_low, grad_context, preferred_element_type=jnp.float32
        )
        return ((grad_keys, grad_values), grad_query)

    zero_state = jnp.zeros(queries.shape, jnp.float32)
    block_numbers = jnp.arange(total_rows // block_rows, dtype=jnp.int32)
    (grad_keys, grad_values), grad_queries = lax.scan(
        backward_block, (zero_state, zero_state), (block_numbers, logsums)
    )
    return jnp.stack([grad_queries.reshape(queries.shape), grad_keys, grad_values], axis=1)


def adam_step(weight, momentum, variance, gradient, rate_value, decay_value):
    momentum_new = beta_one * momentum + (1.0 - beta_one) * gradient
    variance_new = beta_two * variance + (1.0 - beta_two) * gradient * gradient
    direction = (
        momentum_new
        / (1.0 - beta_one**STEP)
        / (jnp.sqrt(variance_new / (1.0 - beta_two**STEP)) + adam_eps)
    )
    return (weight - rate_value * (direction + decay_value * weight), momentum_new, variance_new)


def my_share(array_item, share_index, share_count, dim):
    width = array_item.shape[dim] // share_count
    return lax.dynamic_slice_in_dim(array_item, share_index * width, width, dim)


def share_step(
    weight, momentum, variance, gradient, rate_value, decay_value, share_index, share_count, dim
):
    return adam_step(
        my_share(weight, share_index, share_count, dim),
        my_share(momentum, share_index, share_count, dim),
        my_share(variance, share_index, share_count, dim),
        gradient,
        rate_value,
        decay_value,
    )


def on_device(
    tokens,
    cotangent,
    lengths,
    triple_weight,
    triple_momentum,
    triple_variance,
    merge_weight,
    merge_momentum,
    merge_variance,
    expand_weight,
    expand_momentum,
    expand_variance,
    shrink_weight,
    shrink_momentum,
    shrink_variance,
    vector_weight,
    vector_momentum,
    vector_variance,
):
    total_rows = tokens.shape[0]
    model_width = tokens.shape[1]
    triple_shard = triple_weight.astype(jnp.bfloat16)
    merge_shard = merge_weight.astype(jnp.bfloat16)
    expand_shard = expand_weight.astype(jnp.bfloat16)
    shrink_shard = shrink_weight.astype(jnp.bfloat16)
    vector_shard = vector_weight.astype(jnp.bfloat16)
    triple_low, merge_low, expand_low, shrink_low, vectors_low = (
        lax.all_gather(triple_shard, "fsdp", axis=0, tiled=True),
        lax.all_gather(merge_shard, "fsdp", axis=0, tiled=True),
        lax.all_gather(expand_shard, "fsdp", axis=0, tiled=True),
        lax.all_gather(shrink_shard, "fsdp", axis=0, tiled=True),
        lax.all_gather(vector_shard, "fsdp", axis=1, tiled=True),
    )
    vectors = vectors_low.astype(jnp.float32)
    segment, live_rows = segments_of(lengths[0], total_rows)
    inputs_float = tokens.astype(jnp.float32)
    norm_one, pull_one = jax.vjp(layer_norm, inputs_float, vectors[0], vectors[1])
    norm_one_low = norm_one.astype(jnp.bfloat16)
    bias_triple = jnp.concatenate([vectors[2], jnp.zeros_like(vectors[2]), vectors[3]])
    mixed = jnp.dot(norm_one_low, triple_low, preferred_element_type=jnp.float32) + bias_triple
    mixed_low = mixed.astype(jnp.bfloat16).reshape(total_rows, 3, HEADS, HEAD_DIM)
    queries = mixed_low[:, 0]
    keys_low = mixed_low[:, 1]
    values_low = mixed_low[:, 2]
    context, logsums = attend_forward(queries, keys_low, values_low, segment)
    context_low = context.reshape(total_rows, model_width).astype(jnp.bfloat16)
    residual = (
        inputs_float
        + jnp.dot(context_low, merge_low, preferred_element_type=jnp.float32)
        + vectors[4]
    )
    norm_two, pull_two = jax.vjp(layer_norm, residual, vectors[5], vectors[6])
    norm_two_low = norm_two.astype(jnp.bfloat16)
    expanded = jnp.dot(norm_two_low, expand_low, preferred_element_type=jnp.float32) + vectors[
        8:12
    ].reshape(-1)
    activated, pull_gelu = jax.vjp(gelu_tanh, expanded)
    activated_low = activated.astype(jnp.bfloat16)
    layer_output = (
        residual
        + jnp.dot(activated_low, shrink_low, preferred_element_type=jnp.float32)
        + vectors[7]
    ).astype(jnp.bfloat16)
    triple_low, merge_low, expand_low, shrink_low = (
        lax.all_gather(triple_shard, "fsdp", axis=0, tiled=True),
        lax.all_gather(merge_shard, "fsdp", axis=0, tiled=True),
        lax.all_gather(expand_shard, "fsdp", axis=0, tiled=True),
        lax.all_gather(shrink_shard, "fsdp", axis=0, tiled=True),
    )
    grad_output = cotangent.astype(jnp.float32) * live_rows[:, None]
    grad_output_low = grad_output.astype(jnp.bfloat16)
    grad_shrink = inner_rows(activated_low, grad_output_low)
    bias_shrink = jnp.sum(grad_output_low, axis=0, dtype=jnp.float32)
    grad_active = times_transposed(grad_output_low, shrink_low)
    grad_expanded_low = pull_gelu(grad_active)[0].astype(jnp.bfloat16)
    grad_expand = inner_rows(norm_two_low, grad_expanded_low)
    bias_expand = jnp.sum(grad_expanded_low, axis=0, dtype=jnp.float32)
    grad_norm_two = times_transposed(grad_expanded_low, expand_low)
    grad_residual_norm, gain_two, shift_two = pull_two(grad_norm_two)
    grad_residual = grad_output + grad_residual_norm
    grad_residual_low = grad_residual.astype(jnp.bfloat16)
    grad_merge = inner_rows(context_low, grad_residual_low)
    bias_merge = jnp.sum(grad_residual_low, axis=0, dtype=jnp.float32)
    grad_context_low = (
        times_transposed(grad_residual_low, merge_low)
        .astype(jnp.bfloat16)
        .reshape(total_rows, HEADS, HEAD_DIM)
    )
    grad_mixed = attend_backward(queries, keys_low, values_low, logsums, grad_context_low, segment)
    grad_mixed_low = grad_mixed.reshape(total_rows, 3 * model_width).astype(jnp.bfloat16)
    grad_triple = inner_rows(norm_one_low, grad_mixed_low)
    bias_query = jnp.sum(grad_mixed_low[:, :model_width], axis=0, dtype=jnp.float32)
    bias_value = jnp.sum(grad_mixed_low[:, 2 * model_width :], axis=0, dtype=jnp.float32)
    grad_norm_one = times_transposed(grad_mixed_low, triple_low)
    grad_input_norm, gain_one, shift_one = pull_one(grad_norm_one)
    input_grad = (grad_residual + grad_input_norm).astype(jnp.bfloat16)
    grad_vector = jnp.concatenate(
        [
            jnp.stack(
                [
                    gain_one,
                    shift_one,
                    bias_query,
                    bias_value,
                    bias_merge,
                    gain_two,
                    shift_two,
                    bias_shrink,
                ]
            ),
            bias_expand.reshape(4, model_width),
        ],
        axis=0,
    )
    owned_triple, owned_merge, owned_expand, owned_shrink, owned_vector = (
        lax.psum_scatter(grad_triple, "fsdp", scatter_dimension=0, tiled=True),
        lax.psum_scatter(grad_merge, "fsdp", scatter_dimension=0, tiled=True),
        lax.psum_scatter(grad_expand, "fsdp", scatter_dimension=0, tiled=True),
        lax.psum_scatter(grad_shrink, "fsdp", scatter_dimension=0, tiled=True),
        lax.psum_scatter(grad_vector, "fsdp", scatter_dimension=1, tiled=True),
    )
    total_triple, total_merge, total_expand, total_shrink, total_vector = (
        lax.psum_scatter(owned_triple, "dp", scatter_dimension=1, tiled=True),
        lax.psum_scatter(owned_merge, "dp", scatter_dimension=1, tiled=True),
        lax.psum_scatter(owned_expand, "dp", scatter_dimension=1, tiled=True),
        lax.psum_scatter(owned_shrink, "dp", scatter_dimension=1, tiled=True),
        lax.psum_scatter(owned_vector, "dp", scatter_dimension=0, tiled=True),
    )
    share_index = lax.axis_index("dp")
    share_count = lax.axis_size("dp")
    triple_part = share_step(
        triple_weight,
        triple_momentum,
        triple_variance,
        total_triple,
        rate_matrix,
        decay_matrix,
        share_index,
        share_count,
        1,
    )
    merge_part = share_step(
        merge_weight,
        merge_momentum,
        merge_variance,
        total_merge,
        rate_matrix,
        decay_matrix,
        share_index,
        share_count,
        1,
    )
    expand_part = share_step(
        expand_weight,
        expand_momentum,
        expand_variance,
        total_expand,
        rate_matrix,
        decay_matrix,
        share_index,
        share_count,
        1,
    )
    shrink_part = share_step(
        shrink_weight,
        shrink_momentum,
        shrink_variance,
        total_shrink,
        rate_matrix,
        decay_matrix,
        share_index,
        share_count,
        1,
    )
    vector_part = share_step(
        vector_weight,
        vector_momentum,
        vector_variance,
        total_vector,
        rate_vector,
        0.0,
        share_index,
        share_count,
        0,
    )
    updated = (
        lax.all_gather(triple_part[0], "dp", axis=1, tiled=True),
        lax.all_gather(triple_part[1], "dp", axis=1, tiled=True),
        lax.all_gather(triple_part[2], "dp", axis=1, tiled=True),
        lax.all_gather(merge_part[0], "dp", axis=1, tiled=True),
        lax.all_gather(merge_part[1], "dp", axis=1, tiled=True),
        lax.all_gather(merge_part[2], "dp", axis=1, tiled=True),
        lax.all_gather(expand_part[0], "dp", axis=1, tiled=True),
        lax.all_gather(expand_part[1], "dp", axis=1, tiled=True),
        lax.all_gather(expand_part[2], "dp", axis=1, tiled=True),
        lax.all_gather(shrink_part[0], "dp", axis=1, tiled=True),
        lax.all_gather(shrink_part[1], "dp", axis=1, tiled=True),
        lax.all_gather(shrink_part[2], "dp", axis=1, tiled=True),
        lax.all_gather(vector_part[0], "dp", axis=0, tiled=True),
        lax.all_gather(vector_part[1], "dp", axis=0, tiled=True),
        lax.all_gather(vector_part[2], "dp", axis=0, tiled=True),
    )
    return (layer_output, input_grad) + tuple(updated)


def solution(mesh):
    in_specs = (
        P(("dp", "fsdp"), None),
        P(("dp", "fsdp"), None),
        P(("dp", "fsdp"), None),
        P("fsdp", None),
        P("fsdp", None),
        P("fsdp", None),
        P("fsdp", None),
        P("fsdp", None),
        P("fsdp", None),
        P("fsdp", None),
        P("fsdp", None),
        P("fsdp", None),
        P("fsdp", None),
        P("fsdp", None),
        P("fsdp", None),
        P(None, "fsdp"),
        P(None, "fsdp"),
        P(None, "fsdp"),
    )
    out_specs = (
        P(("dp", "fsdp"), None),
        P(("dp", "fsdp"), None),
        P("fsdp", None),
        P("fsdp", None),
        P("fsdp", None),
        P("fsdp", None),
        P("fsdp", None),
        P("fsdp", None),
        P("fsdp", None),
        P("fsdp", None),
        P("fsdp", None),
        P("fsdp", None),
        P("fsdp", None),
        P("fsdp", None),
        P(None, "fsdp"),
        P(None, "fsdp"),
        P(None, "fsdp"),
    )
    return jax.shard_map(
        on_device, mesh=mesh, in_specs=in_specs, out_specs=out_specs, check_vma=False
    )
```

profile of v0, /device:TPU:0, one launch (start us, length us, event | category | flops | bytes accessed | tf_op | source)
XLA Modules:
  0.0 1706.0 jit_solution(2769178748422125734)
XLA Ops:
  14.4 42.8 %all-gather = bf16[16,68,12]{1,2,0:T(8,128)(2,1)S(1)} all-gather(bf16[1,68,12]{1,2,0:T(8,128)(2,1)S(1)} %convert_bitcast_fusion.3), channel_id=1, replica_groups=mesh['dp'=2,'fsdp'=16] {'fsdp'}, dimensions={0}, use_global_device_ids=true | all-gather | bytes 27744 | tf_op jit(solution)/shard_map/all_gather | solution.py:187
  58.9 19.6 %all-gather.37.cloned.1.call-done = bf16[16,68,1088]{2,1,0:T(8,128)(2,1)} async-done(((bf16[1,68,1088]{2,1,0:T(8,128)(2,1)}), bf16[16,68,1088]{2,1,0:T(8,128)(2,1)}) %all-gather.37.cloned.1.call-update) | async-done | bytes 2367504 | tf_op jit(solution)/shard_map/all_gather | solution.py:184
  82.9 104.3 %all-gather.35.cloned.1.call-done = bf16[16,68,3264]{2,1,0:T(8,128)(2,1)} async-done(((bf16[1,68,3264]{2,1,0:T(8,128)(2,1)}), bf16[16,68,3264]{2,1,0:T(8,128)(2,1)}) %all-gather.35.cloned.1.call-update) | async-done | bytes 7102480 | tf_op jit(solution)/shard_map/all_gather | solution.py:183
  187.2 9.5 reshape.195
  196.7 7.2 fusion.3
  210.0 106.6 %all-gather.39.cloned.1.call-done = bf16[16,68,4352]{2,1,0:T(8,128)(2,1)} async-done(((bf16[1,68,4352]{2,1,0:T(8,128)(2,1)}), bf16[16,68,4352]{2,1,0:T(8,128)(2,1)}) %all-gather.39.cloned.1.call-update) | async-done | bytes 9469968 | tf_op jit(solution)/shard_map/all_gather | solution.py:185
  316.6 10.3 reshape.199
  326.9 6.3 convolution_add_fusion
  335.3 9.3 fusion.48
  344.7 101.2 %all-gather.27.cloned.1.call-done = bf16[4352,1088]{1,0:T(8,128)(2,1)} async-done(((bf16[272,1088]{1,0:T(8,128)(2,1)}), bf16[4352,1088]{1,0:T(8,128)(2,1)}) %all-gather.27.cloned.1.call-update) | async-done | bytes 9469968 | tf_op jit(solution)/shard_map/all_gather | solution.py:186
  445.8 7.3 convert_reduce_fusion
  453.2 7.2 multiply_reduce_fusion.1
  475.1 7.4 fusion.68
  482.5 8.4 fusion.71
  491.0 934.8 %fusion.73 = (f32[72,3264]{1,0:T(8,128)}, f32[80,1088]{1,0:T(8,128)}, f32[72,4352]{1,0:T(8,128)}) fusion(f32[1088,3264]{1,0:T(8,128)} %fusion.68, f32[1088,1088]{1,0:T(8,128)} %fusion.80, f32[1088,4352]{1,0:T(8,128)} %fusion.71), kind=kCustom, calls=%all-reduce-scatter.3 | all-reduce-scatter fusion | flops 10166274 | bytes 40421888
  1431.7 21.4 %collective-permute-done.4 = f32[60,4352]{1,0:T(8,128)} collective-permute-done((f32[60,4352]{1,0:T(8,128)}, f32[60,4352]{1,0:T(8,128)}, u32[]{:S(2)}, u32[]{:S(2)}) %collective-permute-start.4) | collective-permute-done | bytes 1044512
  1453.0 9.4 concatenate.10
  1486.3 15.6 collective-permute-done.3
  1501.9 5.4 collective-permute-done.2
  1507.3 6.9 concatenate.9
  1518.0 7.7 concatenate.8
  1537.0 6.1 fusion.72
  1545.7 78.7 %all-reduce.3 = f32[12,1088]{1,0:T(8,128)S(1)} all-reduce(f32[12,1088]{1,0:T(8,128)S(1)} %concatenate.7), channel_id=10, replica_groups=mesh['dp'=2,'fsdp'=16] {'fsdp'}, use_global_device_ids=true, to_apply=%region_30.31.clone | all-reduce | flops 13056 | bytes 104448
  1639.5 10.3 fusion.15
  (220 shorter events, 144.6 us)
Async XLA Ops:
  7.2 71.2 %all-gather.37.cloned.1.call-start = ((), (), s32[]{:S(2)}) async-start(), calls=%async_computation.12 | async-start | bytes 2820096 | tf_op jit(solution)/shard_map/all_gather | solution.py:184
  9.0 178.1 %all-gather.35.cloned.1.call-start = ((), (), s32[]{:S(2)}) async-start(), calls=%async_computation.11 | async-start | bytes 8146944 | tf_op jit(solution)/shard_map/all_gather | solution.py:183
  11.1 305.5 %all-gather.39.cloned.1.call-start = ((), (), s32[]{:S(2)}) async-start(), calls=%async_computation.13 | async-start | bytes 10653696 | tf_op jit(solution)/shard_map/all_gather | solution.py:185
  12.1 46.3 %copy-start.2 = (bf16[256,1088]{0,1:T(8,128)(2,1)S(1)}, bf16[256,1088]{0,1:T(8,128)(2,1)}, u32[]{:S(2)}) copy-start(bf16[256,1088]{0,1:T(8,128)(2,1)} %param.18) | copy-start | bytes 1671172
  12.1 433.7 %all-gather.27.cloned.1.call-start = ((), (), s32[]{:S(2)}) async-start(), calls=%async_computation.5 | async-start | bytes 10653696 | tf_op jit(solution)/shard_map/all_gather | solution.py:186
  13.5 1451.5 %reduce-scatter.21.cloned.1.call-start = ((), (), s32[]{:S(2)}) async-start(), calls=%async_computation.10 | async-start | bytes 21307392 | tf_op jit(solution)/shard_map/reduce_scatter | solution.py:274
  326.9 8.4 copy-start.5
  344.6 1186.4 %reduce-scatter.19.cloned.1.call-start = ((), (), s32[]{:S(2)}) async-start(), calls=%async_computation.6 | async-start | bytes 1880064 | tf_op jit(solution)/shard_map/reduce_scatter | solution.py:280
  1428.1 24.9 %collective-permute-start.4 = (f32[60,4352]{1,0:T(8,128)}, f32[60,4352]{1,0:T(8,128)}, u32[]{:S(2)}, u32[]{:S(2)}) collective-permute-start(f32[60,4352]{1,0:T(8,128)} %slice.77), channel_id=1, source_target_pairs={{0,1},{1,2},{2,3},{3,4},{4,5},{5,6},{6,7},{7,8},{8,9},{9,10},{10,1... | collective-permute-start | bytes 3133448
  1465.0 161.9 %reduce-scatter.27.cloned.1.call-start = ((), (), s32[]{:S(2)}) async-start(), calls=%async_computation.19 | async-start | bytes 2506752
  1468.1 184.5 %reduce-scatter.25.cloned.1.call-start = ((), (), s32[]{:S(2)}) async-start(), calls=%async_computation.18 | async-start | bytes 835584
  1470.3 47.7 %collective-permute-start = (f32[60,3264]{1,0:T(8,128)}, f32[60,3264]{1,0:T(8,128)}, u32[]{:S(2)}, u32[]{:S(2)}) collective-permute-start(f32[60,3264]{1,0:T(8,128)} %slice.75), channel_id=1, source_target_pairs={{0,1},{1,2},{2,3},{3,4},{4,5},{5,6},{6,7},{7,8},{8,9},{9,10},{10,1... | collective-permute-start | bytes 2350088
  1475.6 31.7 %collective-permute-start.2 = (f32[80,1088]{1,0:T(8,128)}, f32[80,1088]{1,0:T(8,128)}, u32[]{:S(2)}, u32[]{:S(2)}) collective-permute-start(f32[80,1088]{1,0:T(8,128)} %get-tuple-element.89), channel_id=1, source_target_pairs={{0,2},{1,3},{2,4},{3,5},{4,6},{5,7},{6,8},{7,9},{8,10},{9,11},{10,... | collective-permute-start | bytes 1044488
  1477.6 29.7 %collective-permute-start.1 = (f32[80,1088]{1,0:T(8,128)}, f32[80,1088]{1,0:T(8,128)}, u32[]{:S(2)}, u32[]{:S(2)}) collective-permute-start(f32[80,1088]{1,0:T(8,128)} %get-tuple-element.89), channel_id=1, source_target_pairs={{0,1},{1,2},{2,3},{3,4},{4,5},{5,6},{6,7},{7,8},{8,9},{9,10},{10,1... | collective-permute-start | bytes 1044488
  1480.6 21.4 %collective-permute-start.3 = (f32[20,1088]{1,0:T(8,128)S(1)}, f32[20,1088]{1,0:T(8,128)}, u32[]{:S(2)}, u32[]{:S(2)}) collective-permute-start(f32[20,1088]{1,0:T(8,128)S(1)} %slice.76), channel_id=1, source_target_pairs={{0,3},{1,4},{2,5},{3,6},{4,7},{5,8},{6,9},{7,10},{8,11},{9,12},{10... | collective-permute-start | bytes 261128
  1518.0 147.1 %reduce-scatter.23.cloned.1.call-start = ((), (), s32[]{:S(2)}) async-start(), calls=%async_computation.17 | async-start | bytes 2506752
  1530.9 151.7 %all-gather.29.cloned.1.call-start = ((), (), s32[]{:S(2)}) async-start(), calls=%async_computation.7 | async-start | bytes 1880064 | tf_op jit(solution)/shard_map/all_gather | solution.py:348
  1534.2 148.4 %all-gather.31.cloned.1.call-start = ((), (), s32[]{:S(2)}) async-start(), calls=%async_computation.8 | async-start | bytes 1880064 | tf_op jit(solution)/shard_map/all_gather | solution.py:349
  1535.0 147.6 %all-gather.33.cloned.1.call-start = ((), (), s32[]{:S(2)}) async-start(), calls=%async_computation.9 | async-start | bytes 1880064 | tf_op jit(solution)/shard_map/all_gather | solution.py:350
  1536.9 145.7 %all-gather.45.cloned.1.call-start = ((), (), s32[]{:S(2)}) async-start(), calls=%async_computation.16 | async-start | bytes 2088960 | tf_op jit(solution)/shard_map/all_gather | solution.py:353
  1632.0 54.5 %all-gather.41.cloned.1.call-start = ((), (), s32[]{:S(2)}) async-start(), calls=%async_computation.14 | async-start | bytes 2088960 | tf_op jit(solution)/shard_map/all_gather | solution.py:351
  1639.5 10.4 copy-start.4
  1639.5 10.4 copy-start.6
  1649.9 40.6 %all-gather.43.cloned.1.call-start = ((), (), s32[]{:S(2)}) async-start(), calls=%async_computation.15 | async-start | bytes 2088960 | tf_op jit(solution)/shard_map/all_gather | solution.py:352
  (26 other events, 72.9 us)
Sparse Core Ops, SparseCore 0:
  11.3 67.1 all-gather.36
  81.8 105.2 all-gather.34
  190.5 126.0 all-gather.38
  319.9 125.9 all-gather.26
  451.6 533.1 reduce-scatter.20
  1465.1 9.7 reduce-scatter.18
  1477.3 10.3 reduce-scatter.26
  1518.1 19.1 reduce-scatter.24
  1539.6 11.6 reduce-scatter.22
  1553.4 10.5 all-gather.28
  1565.6 10.4 all-gather.30
  1577.6 10.4 all-gather.32
  1632.2 7.3 all-gather.44
  1650.0 8.0 all-gather.40
  1660.1 10.8 all-gather.42
where the time goes:
time: 1720 us; the launch traced here: 1710 us
  blocking collectives  1080 us (63%)
  waiting for transfers between devices  375 us (22%)
  local copies, waits for them, and re-layouts  110 us (6%)
  matrix products  82.4 us (5%)
  other arithmetic  24.6 us (1%)
  between operations  17.6 us (1%)
  starting transfers between devices  17.4 us (1%)
    unnamed x3, blocking collectives  1020 us
    all_gather x1, waiting for transfers between devices, on_device(): lax.all_gather(expand_shard, 'fsdp', axis=0, tiled=True)  107 us
    all_gather x1, waiting for transfers between devices, on_device(): lax.all_gather(triple_shard, 'fsdp', axis=0, tiled=True)  104 us
    all_gather x1, waiting for transfers between devices, on_device(): lax.all_gather(shrink_shard, 'fsdp', axis=0, tiled=True)  101 us
    unnamed x96, local copies, waits for them, and re-layouts  101 us
    unnamed x23, waiting for transfers between devices  43.3 us
    all_gather x1, blocking collectives, on_device(): lax.all_gather(vector_shard, 'fsdp', axis=1, tiled=True)  42.8 us
  transfers between devices with their start and end apart: 20, of which 7 were waited for; matrix products, arithmetic and copies ran while one was open for 66% of the time, Pallas kernels for 0%

commit v1 on v0

v1 whole, which is shorter than its diff:
```python
import functools

import jax
import jax.numpy as jnp
from jax import lax
from jax.experimental import pallas as pl
from jax.experimental.pallas import tpu as pltpu
from jax.sharding import PartitionSpec as P

HEADS = 17
HEAD_DIM = 64
STEP = 10
MESH = pl.DeviceIdType.MESH


norm_eps = 1e-05
beta_one = 0.9
beta_two = 0.95
adam_eps = 1e-08
rate_matrix = 0.05
rate_vector = 0.4
decay_matrix = 0.1
masked_score = -1e30


def chip_grid(count):
    side = 1
    while 4 * side * side < count:
        side += 1
    return 4, side, side


def row_split(rows, flip):
    tiles = rows // 16
    first = 16 * ((tiles + 1) // 2 if not flip else tiles // 2)
    return ((0, first), (first, rows - first))


def place(sizes):
    _, size_y, size_x = sizes
    core = lax.axis_index("dp")
    chip = lax.axis_index("fsdp")
    return core, lax.div(chip, size_y * size_x), lax.rem(lax.div(chip, size_x), size_y), lax.rem(chip, size_x)


def greet(sizes, core, z, y, x):
    size_z, size_y, size_x = sizes
    barrier = pltpu.get_barrier_semaphore()
    peers = [(1 - core, chip_id(sizes, z, y, x))]
    peers += [(core, chip_id(sizes, lax.rem(z + d, size_z), y, x)) for d in range(1, size_z)]
    peers += [(core, chip_id(sizes, z, lax.rem(y + d, size_y), x)) for d in range(1, size_y)]
    peers += [(core, chip_id(sizes, z, y, lax.rem(x + d, size_x))) for d in range(1, size_x)]
    for peer in peers:
        pl.semaphore_signal(barrier, inc=1, device_id=peer, device_id_type=MESH)
    pl.semaphore_wait(barrier, len(peers))


def chip_id(sizes, z, y, x):
    return (z * sizes[1] + y) * sizes[2] + x


def remote(src, dst, send_sem, recv_sem, peer):
    return pltpu.make_async_remote_copy(
        src_ref=src, dst_ref=dst, send_sem=send_sem, recv_sem=recv_sem,
        device_id=peer, device_id_type=MESH,
    )


def gather_kernel(sizes, splits, *refs):
    arrays = len(splits)
    ins, outs = refs[: arrays + 1], refs[arrays + 1 : 2 * arrays + 2]
    (local_sem, zs_sem, zr_sem, as_sem, ar_sem, bs_sem, br_sem, ps_sem, pr_sem) = refs[2 * arrays + 2 :]
    size_z, side, _ = sizes
    core, z, y, x = place(sizes)
    greet(sizes, core, z, y, x)

    def run(c):
        def at(second, third):
            return (third, second) if c == 0 else (second, third)

        mine = (x, y) if c == 0 else (y, x)
        sends = []

        def back(d2, d3, own=mine):
            return at(lax.rem(own[0] + side - d2, side), lax.rem(own[1] + side - d3, side))

        def peer_of(d2, d3):
            py, px = at(lax.rem(mine[0] + d2, side), lax.rem(mine[1] + d3, side))
            return (core, chip_id(sizes, z, py, px))

        def line(k, yx):
            if k == arrays:
                return outs[k].at[:, yx[0], yx[1]]
            start, rows = splits[k][c]
            return outs[k].at[:, yx[0], yx[1], pl.ds(start, rows), :]

        def go(copy):
            copy.start()
            sends.append(copy)

        def line_copy(k, yx, ss, rs, peer):
            return remote(line(k, yx), line(k, yx), ss, rs, peer)

        def second_copy(k, d2):
            return line_copy(k, (y, x), as_sem.at[k, d2], ar_sem.at[k, d2], peer_of(d2, 0))

        def third_copy(k, d2, d3):
            return line_copy(k, back(d2, 0), bs_sem.at[k, d2, d3], br_sem.at[k, d2, d3], peer_of(0, d3))

        def partner_copy(k, d2, d3):
            return line_copy(
                k, back(d2, d3), ps_sem.at[k, d2, d3], pr_sem.at[k, d2, d3],
                (1 - core, chip_id(sizes, z, y, x)),
            )

        def block(k):
            if k == arrays:
                return ins[k], outs[k].at[z, y, x]
            start, rows = splits[k][c]
            return ins[k].at[pl.ds(start, rows), :], outs[k].at[z, y, x, pl.ds(start, rows), :]

        def z_copy(k, d):
            src, dst = block(k)
            return remote(
                src, dst, zs_sem.at[k, d], zr_sem.at[k, d],
                (core, chip_id(sizes, lax.rem(z + d, size_z), y, x)),
            )

        def own_copy(k):
            src, dst = block(k)
            return pltpu.make_async_copy(src, dst, local_sem.at[k])

        order = [arrays] + list(range(arrays))
        for k in order:
            own_copy(k).start()
            for d in range(1, size_z):
                go(z_copy(k, d))

        def stage_one(k):
            own_copy(k).wait()
            for d in range(1, size_z):
                z_copy(k, d).wait_recv()
            for d in range(1, side):
                go(second_copy(k, d))
            for d in range(1, side):
                go(third_copy(k, 0, d))
            if k < arrays:
                go(partner_copy(k, 0, 0))

        def stage_two(k):
            for d2 in range(1, side):
                second_copy(k, d2).wait_recv()
                for d3 in range(1, side):
                    go(third_copy(k, d2, d3))
                if k < arrays:
                    go(partner_copy(k, d2, 0))

        def stage_three(k):
            for d3 in range(1, side):
                for d2 in range(side):
                    third_copy(k, d2, d3).wait_recv()
                    if k < arrays:
                        go(partner_copy(k, d2, d3))

        stages = (stage_one, stage_two, stage_three)
        for tick in range(len(order) + len(stages) - 1):
            for s in reversed(range(len(stages))):
                if 0 <= tick - s < len(order):
                    stages[s](order[tick - s])

        theirs = (y, x) if c == 0 else (x, y)
        for k in range(arrays):
            start, rows = splits[k][1 - c]
            for d2 in range(side):
                for d3 in range(side):
                    a = lax.rem(theirs[0] + side - d2, side)
                    b = lax.rem(theirs[1] + side - d3, side)
                    yx = (a, b) if c == 0 else (b, a)
                    ref = outs[k].at[:, yx[0], yx[1], pl.ds(start, rows), :]
                    remote(
                        ref, ref, ps_sem.at[k, d2, d3], pr_sem.at[k, d2, d3],
                        (1 - core, chip_id(sizes, z, y, x)),
                    ).wait_recv()
        for copy in sends:
            copy.wait_send()

    pl.when(core == 0)(lambda: run(0))
    pl.when(core == 1)(lambda: run(1))


def gather_all(sizes, shards, vector_shard):
    arrays = len(shards)
    size_z, side, _ = sizes
    splits = tuple(row_split(s.shape[0], k % 2 == 1) for k, s in enumerate(shards))
    everything = tuple(shards) + (vector_shard,)
    dma = pltpu.SemaphoreType.DMA
    return pl.pallas_call(
        functools.partial(gather_kernel, sizes, splits),
        out_shape=[jax.ShapeDtypeStruct(sizes + s.shape, s.dtype) for s in everything],
        in_specs=[pl.BlockSpec(memory_space=pl.ANY)] * (arrays + 1),
        out_specs=[pl.BlockSpec(memory_space=pl.ANY)] * (arrays + 1),
        scratch_shapes=[
            dma((arrays + 1,)),
            dma((arrays + 1, size_z)), dma((arrays + 1, size_z)),
            dma((arrays + 1, side)), dma((arrays + 1, side)),
            dma((arrays + 1, side, side)), dma((arrays + 1, side, side)),
            dma((arrays, side, side)), dma((arrays, side, side)),
        ],
        compiler_params=pltpu.CompilerParams(collective_id=0, has_side_effects=True),
    )(*everything)


def add_into(total, first, extra, blocks):
    counts = list(blocks)
    steps = 1
    for count in counts:
        steps *= count

    def body(step, carry):
        index = []
        for count in reversed(counts):
            index.append(lax.rem(step, count))
            step = lax.div(step, count)
        index = tuple(reversed(index))
        value = first(index)[...].astype(jnp.float32) + extra(index)[...].astype(jnp.float32)
        total(index)[...] = value.astype(total(index).dtype)
        return carry

    lax.fori_loop(0, steps, body, 0)


def scatter_kernel(sizes, splits, *refs):
    arrays = len(splits)
    ins, vec_in = refs[:arrays], refs[arrays]
    outs, vec_out = refs[arrays + 1 : 2 * arrays + 1], refs[2 * arrays + 1]
    (own, part, second, third, fourth, result, vec_slots,
     load_sem, store_sem, as_sem, ar_sem, bs_sem, br_sem, cs_sem, cr_sem, ds_sem, dr_sem,
     es_sem, er_sem, vs_sem, vr_sem, credit) = refs[2 * arrays + 2 :]
    size_z, side, _ = sizes
    core, z, y, x = place(sizes)
    greet(sizes, core, z, y, x)
    partner = (1 - core, chip_id(sizes, z, y, x))

    def run(c):
        sends = []

        def go(copy):
            copy.start()
            sends.append(copy)

        def rows_of(k, which):
            start, rows = splits[k][which]
            return pl.ds(start, rows)

        def height(k, which=c):
            return pl.ds(0, splits[k][which][1])

        def load(k):
            return pltpu.make_async_copy(
                ins[k].at[:, :, :, rows_of(k, c), :], own.at[k, :, :, :, height(k), :], load_sem.at[k]
            )

        def swap(k):
            return remote(
                ins[k].at[:, :, :, rows_of(k, 1 - c), :],
                part.at[k % 2, :, :, :, height(k, 1 - c), :],
                as_sem.at[k], ar_sem.at[k], partner,
            )

        def swapped(k):
            ref = part.at[k % 2, :, :, :, height(k), :]
            return remote(ref, ref, as_sem.at[k], ar_sem.at[k], partner)

        def along(first, d):
            if first == (c == 0):
                other = lax.rem(y + d, side)
                return other, x, (core, chip_id(sizes, z, other, x))
            other = lax.rem(x + d, side)
            return y, other, (core, chip_id(sizes, z, y, other))

        def copy_b(k, d):
            py, px, peer = along(True, d)
            src = own.at[k, :, py, :, height(k), :] if c == 0 else own.at[k, :, :, px, height(k), :]
            return remote(src, second.at[k, d - 1, :, :, height(k), :], bs_sem.at[k, d], br_sem.at[k, d], peer)

        def copy_c(k, d):
            py, px, peer = along(False, d)
            return remote(
                own.at[k, :, py, px, height(k), :], third.at[k, d - 1, :, height(k), :],
                cs_sem.at[k, d], cr_sem.at[k, d], peer,
            )

        def copy_d(k, d):
            pz = lax.rem(z + d, size_z)
            return remote(
                own.at[k, pz, y, x, height(k), :], fourth.at[k, d - 1, height(k), :],
                ds_sem.at[k, d], dr_sem.at[k, d], (core, chip_id(sizes, pz, y, x)),
            )

        def stage_a(k):
            load(k).wait()
            swapped(k).wait_recv()
            h = height(k)
            add_into(
                lambda i: own.at[k, i[0], i[1], i[2], h, :],
                lambda i: own.at[k, i[0], i[1], i[2], h, :],
                lambda i: part.at[k % 2, i[0], i[1], i[2], h, :],
                sizes,
            )
            if k + 2 < arrays:
                pl.semaphore_signal(credit, inc=1, device_id=partner, device_id_type=MESH)
            for d in range(1, side):
                go(copy_b(k, d))
            if k + 2 < arrays:
                pl.semaphore_wait(credit, 1)
                go(swap(k + 2))

        def stage_b(k):
            h = height(k)
            for d in range(1, side):
                copy_b(k, d).wait_recv()

                def mine(i):
                    if c == 0:
                        return own.at[k, i[0], y, i[1], h, :]
                    return own.at[k, i[0], i[1], x, h, :]

                add_into(mine, mine, lambda i: second.at[k, d - 1, i[0], i[1], h, :], (size_z, side))
            for d in range(1, side):
                go(copy_c(k, d))

        def stage_c(k):
            h = height(k)
            for d in range(1, side):
                copy_c(k, d).wait_recv()

                def mine(i):
                    return own.at[k, i[0], y, x, h, :]

                add_into(mine, mine, lambda i: third.at[k, d - 1, i[0], h, :], (size_z,))
            for d in range(1, size_z):
                go(copy_d(k, d))

        def finish(k):
            return remote(
                result.at[k, height(k), :], outs[k].at[rows_of(k, c), :], es_sem.at[k], er_sem.at[k], partner
            )

        def store(k):
            return pltpu.make_async_copy(
                result.at[k, height(k), :], outs[k].at[rows_of(k, c), :], store_sem.at[k]
            )

        def stage_d(k):
            h = height(k)
            total = own[k, z, y, x, h, :].astype(jnp.float32)
            for d in range(1, size_z):
                copy_d(k, d).wait_recv()
                total = total + fourth[k, d - 1, h, :].astype(jnp.float32)
            result[k, h, :] = total
            store(k).start()
            go(finish(k))

        vec_steps = (
            (2, core, lambda i: (i, chip_id(sizes, z, y, x))),
            (side, y, lambda i: (core, chip_id(sizes, z, i, x))),
            (side, x, lambda i: (core, chip_id(sizes, z, y, i))),
            (size_z, z, lambda i: (core, chip_id(sizes, i, y, x))),
        )

        def vec_copy(step, d):
            count, where, peer = vec_steps[step]
            slot = vec_slots.at[step, where]
            return remote(
                slot, slot, vs_sem.at[step, d], vr_sem.at[step, d], peer(lax.rem(where + d, count))
            )

        def vec_arrived(step, d):
            count, where, peer = vec_steps[step]
            source = lax.rem(where + count - d, count)
            slot = vec_slots.at[step, source]
            return remote(slot, slot, vs_sem.at[step, d], vr_sem.at[step, d], peer(lax.rem(where + d, count)))

        def vec_send(step, value):
            count, where, _ = vec_steps[step]
            vec_slots[step, where] = value
            for d in range(1, count):
                go(vec_copy(step, d))

        def vec_sum(step):
            count = vec_steps[step][0]
            for d in range(1, count):
                vec_arrived(step, d).wait_recv()
            total = vec_slots[step, 0]
            for i in range(1, count):
                total = total + vec_slots[step, i]
            return total

        for k in range(arrays):
            load(k).start()
        for k in range(min(2, arrays)):
            go(swap(k))
        vec_send(0, vec_in[...])

        stages = (stage_a, stage_b, stage_c, stage_d)
        for tick in range(arrays + len(stages) - 1):
            for s in reversed(range(len(stages))):
                if 0 <= tick - s < arrays:
                    stages[s](tick - s)
            if tick < 3:
                vec_send(tick + 1, vec_sum(tick))
            elif tick == 3:
                vec_out[...] = vec_sum(3)

        for k in range(arrays):
            store(k).wait()
            start, rows = splits[k][1 - c]
            ref = outs[k].at[pl.ds(start, rows), :]
            remote(ref, ref, es_sem.at[k], er_sem.at[k], partner).wait_recv()
        for copy in sends:
            copy.wait_send()

    pl.when(core == 0)(lambda: run(0))
    pl.when(core == 1)(lambda: run(1))


def scatter_all(sizes, terms, vector_term):
    arrays = len(terms)
    size_z, side, _ = sizes
    rows, width = terms[0].shape[-2:]
    splits = tuple(row_split(rows, k % 2 == 1) for k in range(arrays))
    most = max(part[1] for split in splits for part in split)
    dma = pltpu.SemaphoreType.DMA
    low = jnp.bfloat16
    pair = [dma((arrays,)), dma((arrays,))]
    sides = [dma((arrays, side)), dma((arrays, side))]
    return pl.pallas_call(
        functools.partial(scatter_kernel, sizes, splits),
        out_shape=[jax.ShapeDtypeStruct((rows, width), jnp.float32) for _ in terms]
        + [jax.ShapeDtypeStruct(vector_term.shape, jnp.float32)],
        in_specs=[pl.BlockSpec(memory_space=pl.ANY)] * arrays
        + [pl.BlockSpec(memory_space=pltpu.VMEM)],
        out_specs=[pl.BlockSpec(memory_space=pl.ANY)] * arrays
        + [pl.BlockSpec(memory_space=pltpu.VMEM)],
        scratch_shapes=[
            pltpu.VMEM((arrays,) + sizes + (most, width), low),
            pltpu.VMEM((2,) + sizes + (most, width), low),
            pltpu.VMEM((arrays, side - 1, size_z, side, most, width), low),
            pltpu.VMEM((arrays, side - 1, size_z, most, width), low),
            pltpu.VMEM((arrays, size_z - 1, most, width), low),
            pltpu.VMEM((arrays, most, width), jnp.float32),
            pltpu.VMEM((4, max(size_z, side)) + vector_term.shape, jnp.float32),
            dma((arrays,)), dma((arrays,)),
        ]
        + pair + sides + sides
        + [dma((arrays, size_z)), dma((arrays, size_z))]
        + pair
        + [dma((4, max(size_z, side))), dma((4, max(size_z, side)))]
        + [pltpu.SemaphoreType.REGULAR],
        compiler_params=pltpu.CompilerParams(
            collective_id=1, has_side_effects=True, vmem_limit_bytes=60 * 1024 * 1024
        ),
    )(*terms, vector_term)


def layer_norm(values, gain_row, shift_row):
    center = values - jnp.mean(values, axis=-1, keepdims=True)
    spread = jnp.mean(center * center, axis=-1, keepdims=True)
    return center * lax.rsqrt(spread + norm_eps) * gain_row + shift_row


def gelu_tanh(values):
    return jax.nn.gelu(values, approximate=True)


def segments_of(length_row, total_rows):
    places = jnp.arange(total_rows, dtype=jnp.int32)
    bounds = jnp.cumsum(length_row)
    segment = jnp.sum((places[:, None] >= bounds[None, :]).astype(jnp.int32), axis=1)
    live_rows = (places < bounds[-1]).astype(jnp.float32)
    return (segment, live_rows)


def dot_low(left_side, right_side):
    return jnp.dot(left_side, right_side, preferred_element_type=jnp.float32)


def inner_rows(left_side, right_side):
    return lax.dot_general(
        left_side, right_side, (((0,), (0,)), ((), ())), preferred_element_type=jnp.float32
    )


def times_transposed(left_side, right_side):
    return lax.dot_general(
        left_side, right_side, (((1,), (1,)), ((), ())), preferred_element_type=jnp.float32
    )


def attend_forward(queries, keys_low, values_low, segment):
    total_rows = queries.shape[0]
    places = jnp.arange(total_rows, dtype=jnp.int32)
    allowed = (segment[:, None] == segment[None, :]) & (places[None, :] <= places[:, None])
    scores = jnp.einsum("qhe,khe->hqk", queries, keys_low, preferred_element_type=jnp.float32)
    scores = jnp.where(allowed[None], scores * (HEAD_DIM**-0.5), masked_score)
    weights = jnp.exp(scores - jnp.max(scores, axis=-1, keepdims=True))
    probability = weights / jnp.sum(weights, axis=-1, keepdims=True)
    probs_low = probability.astype(jnp.bfloat16)
    context = jnp.einsum("hqk,khe->qhe", probs_low, values_low, preferred_element_type=jnp.float32)
    return context, probability


def attend_backward(queries, keys_low, values_low, probability, grad_context):
    scaling = HEAD_DIM**-0.5
    probs_low = probability.astype(jnp.bfloat16)
    grad_probs = jnp.einsum(
        "qhe,khe->hqk", grad_context, values_low, preferred_element_type=jnp.float32
    )
    centered = grad_probs - jnp.sum(grad_probs * probability, axis=-1, keepdims=True)
    grad_scores = (probability * centered).astype(jnp.bfloat16)
    grad_query = jnp.einsum("hqk,khe->qhe", grad_scores, keys_low, preferred_element_type=jnp.float32)
    grad_keys = jnp.einsum("hqk,qhe->khe", grad_scores, queries, preferred_element_type=jnp.float32)
    grad_values = jnp.einsum(
        "hqk,qhe->khe", probs_low, grad_context, preferred_element_type=jnp.float32
    )
    return grad_query * scaling, grad_keys * scaling, grad_values


def adam_step(weight, momentum, variance, gradient, rate_value, decay_value):
    momentum_new = beta_one * momentum + (1.0 - beta_one) * gradient
    variance_new = beta_two * variance + (1.0 - beta_two) * gradient * gradient
    direction = (
        momentum_new
        / (1.0 - beta_one**STEP)
        / (jnp.sqrt(variance_new / (1.0 - beta_two**STEP)) + adam_eps)
    )
    return (weight - rate_value * (direction + decay_value * weight), momentum_new, variance_new)


def on_device(
    sizes,
    tokens,
    cotangent,
    lengths,
    triple_weight,
    triple_momentum,
    triple_variance,
    merge_weight,
    merge_momentum,
    merge_variance,
    expand_weight,
    expand_momentum,
    expand_variance,
    shrink_weight,
    shrink_momentum,
    shrink_variance,
    vector_weight,
    vector_momentum,
    vector_variance,
):
    total_rows, width = tokens.shape
    low = jnp.bfloat16
    rows = merge_weight.shape[0]
    count = sizes[0] * sizes[1] * sizes[2]
    blocks = expand_weight.shape[1] // width
    padding = -(blocks * rows) % 16

    def columns(array_item, parts):
        return [array_item[:, i * width : (i + 1) * width] for i in range(parts)]

    def packed(parts):
        whole = jnp.concatenate([p.astype(low) for p in parts], axis=0)
        return jnp.pad(whole, ((0, padding), (0, 0)))

    shards = (
        packed(columns(triple_weight, 3) + [merge_weight]),
        packed(columns(expand_weight, blocks)),
        packed([shrink_weight]),
    )
    all_low = gather_all(sizes, shards, vector_weight.astype(low))

    def unpacked(array_item):
        array_item = array_item.reshape(count, -1, width)
        return [
            array_item[:, i * rows : (i + 1) * rows].reshape(count * rows, width)
            for i in range(blocks)
        ]

    query_low, key_low, value_low, merge_low = unpacked(all_low[0])
    expand_low = unpacked(all_low[1])
    shrink_low = all_low[2].reshape(count, -1, width)[:, : blocks * rows].reshape(-1, width)
    vectors_low = all_low[3].reshape(count, vector_weight.shape[0], rows)
    vectors = vectors_low.transpose(1, 0, 2).reshape(-1, width).astype(jnp.float32)

    segment, live_rows = segments_of(lengths[0], total_rows)
    inputs_float = tokens.astype(jnp.float32)
    norm_one, pull_one = jax.vjp(layer_norm, inputs_float, vectors[0], vectors[1])
    norm_one_low = norm_one.astype(low)
    heads = (total_rows, HEADS, HEAD_DIM)
    queries = (dot_low(norm_one_low, query_low) + vectors[2]).astype(low).reshape(heads)
    keys_low = dot_low(norm_one_low, key_low).astype(low).reshape(heads)
    values_low = (dot_low(norm_one_low, value_low) + vectors[3]).astype(low).reshape(heads)
    context, probability = attend_forward(queries, keys_low, values_low, segment)
    context_low = context.reshape(total_rows, width).astype(low)
    residual = inputs_float + dot_low(context_low, merge_low) + vectors[4]
    norm_two, pull_two = jax.vjp(layer_norm, residual, vectors[5], vectors[6])
    norm_two_low = norm_two.astype(low)
    pulls, activated_low = [], []
    for i in range(blocks):
        activated, pull_gelu = jax.vjp(
            gelu_tanh, dot_low(norm_two_low, expand_low[i]) + vectors[8 + i]
        )
        pulls.append(pull_gelu)
        activated_low.append(activated.astype(low))
    activated_low = jnp.concatenate(activated_low, axis=1)
    layer_output = (residual + dot_low(activated_low, shrink_low) + vectors[7]).astype(low)

    grad_output = cotangent.astype(jnp.float32) * live_rows[:, None]
    grad_output_low = grad_output.astype(low)
    grad_shrink = inner_rows(activated_low, grad_output_low)
    bias_shrink = jnp.sum(grad_output_low, axis=0, dtype=jnp.float32)
    grad_norm_two, grad_expand, bias_expand = 0.0, [], []
    for i in range(blocks):
        grad_active = times_transposed(grad_output_low, shrink_low[i * width : (i + 1) * width])
        grad_expanded_low = pulls[i](grad_active)[0].astype(low)
        grad_expand.append(inner_rows(norm_two_low, grad_expanded_low))
        bias_expand.append(jnp.sum(grad_expanded_low, axis=0, dtype=jnp.float32))
        grad_norm_two = grad_norm_two + times_transposed(grad_expanded_low, expand_low[i])
    grad_residual_norm, gain_two, shift_two = pull_two(grad_norm_two)
    grad_residual = grad_output + grad_residual_norm
    grad_residual_low = grad_residual.astype(low)
    grad_merge = inner_rows(context_low, grad_residual_low)
    bias_merge = jnp.sum(grad_residual_low, axis=0, dtype=jnp.float32)
    grad_context_low = times_transposed(grad_residual_low, merge_low).astype(low).reshape(heads)
    grad_mixed = attend_backward(queries, keys_low, values_low, probability, grad_context_low)
    grad_mixed_low = [g.reshape(total_rows, width).astype(low) for g in grad_mixed]
    grad_triple = [inner_rows(norm_one_low, g) for g in grad_mixed_low]
    bias_query = jnp.sum(grad_mixed_low[0], axis=0, dtype=jnp.float32)
    bias_value = jnp.sum(grad_mixed_low[2], axis=0, dtype=jnp.float32)
    grad_norm_one = (
        times_transposed(grad_mixed_low[0], query_low)
        + times_transposed(grad_mixed_low[1], key_low)
        + times_transposed(grad_mixed_low[2], value_low)
    )
    grad_input_norm, gain_one, shift_one = pull_one(grad_norm_one)
    input_grad = (grad_residual + grad_input_norm).astype(low)
    grad_vector = jnp.stack(
        [gain_one, shift_one, bias_query, bias_value, bias_merge, gain_two, shift_two, bias_shrink]
        + bias_expand
    )

    def spread(parts):
        whole = jnp.concatenate([p.astype(low).reshape(count, -1, width) for p in parts], axis=1)
        whole = jnp.pad(whole, ((0, 0), (0, padding), (0, 0)))
        return whole.reshape(sizes + whole.shape[1:])

    owned_first, owned_expand, owned_shrink, total_vector = scatter_all(
        sizes,
        (spread(grad_triple + [grad_merge]), spread(grad_expand), spread([grad_shrink])),
        grad_vector,
    )

    def beside(array_item, first, parts):
        return jnp.concatenate(
            [array_item[i * rows : (i + 1) * rows] for i in range(first, first + parts)], axis=1
        )

    owned_vector = lax.dynamic_slice_in_dim(total_vector, lax.axis_index("fsdp") * rows, rows, 1)
    triple_part = adam_step(
        triple_weight, triple_momentum, triple_variance, beside(owned_first, 0, 3),
        rate_matrix, decay_matrix,
    )
    merge_part = adam_step(
        merge_weight, merge_momentum, merge_variance, beside(owned_first, 3, 1),
        rate_matrix, decay_matrix,
    )
    expand_part = adam_step(
        expand_weight, expand_momentum, expand_variance, beside(owned_expand, 0, blocks),
        rate_matrix, decay_matrix,
    )
    shrink_part = adam_step(
        shrink_weight, shrink_momentum, shrink_variance, owned_shrink[: blocks * rows],
        rate_matrix, decay_matrix,
    )
    vector_part = adam_step(
        vector_weight, vector_momentum, vector_variance, owned_vector, rate_vector, 0.0
    )
    return (
        (layer_output, input_grad) + triple_part + merge_part + expand_part + shrink_part + vector_part
    )


def solution(mesh):
    token_spec, matrix_spec, vector_spec = P(("dp", "fsdp"), None), P("fsdp", None), P(None, "fsdp")
    return jax.shard_map(
        functools.partial(on_device, chip_grid(mesh.shape["fsdp"])),
        mesh=mesh,
        in_specs=(token_spec,) * 3 + (matrix_spec,) * 12 + (vector_spec,) * 3,
        out_specs=(token_spec,) * 2 + (matrix_spec,) * 12 + (vector_spec,) * 3,
        check_vma=False,
    )
```

time: 1720 us -> 617 us (0.36)
  blocking collectives: 1080 us -> 0 us
  waiting for transfers between devices: 375 us -> 0 us
  Pallas kernels: 0 us -> 350 us
  other arithmetic: 24.6 us -> 47.7 us
  matrix products: 82.4 us -> 103 us
  starting transfers between devices: 17.4 us -> 0 us
    unnamed x3 -> x0, blocking collectives: 1020 us -> none
    pallas_call x0 -> x2, Pallas kernels: none -> 350 us  [the longest x1 183 us: scatter_all(): pl.pallas_call(functools.partial(scatter_kernel, sizes, splits), out_shap...]
    all_gather x10 -> x0, waiting for transfers between devices: 332 us -> none  [the longest x1 107 us: on_device(): lax.all_gather(expand_shard, 'fsdp', axis=0, tiled=True)]
    unnamed x96 -> x114, local copies, waits for them, and re-layouts: 101 us -> 7.21 us
    all_gather x10 -> x0, blocking collectives: 63 us -> none  [the longest x1 42.8 us: on_device(): lax.all_gather(vector_shard, 'fsdp', axis=1, tiled=True)]
    unnamed x23 -> x0, waiting for transfers between devices: 43.3 us -> none
    reshape x1 -> x8, local copies, waits for them, and re-layouts: 0.08 us -> 32.4 us  [unpacked(): array_item[:, i * rows:(i + 1) * rows].reshape(count * rows, width)]
    concatenate x2 -> x10, local copies, waits for them, and re-layouts: 0.16 us -> 32.5 us  [the longest x8 30.8 us: spread(): jnp.concatenate([p.astype(low).reshape(count, -1, width) for p in parts],...]
  transfers between devices with their start and end apart: 20 -> 0, of which waited for: 7 -> 0; matrix products, arithmetic and copies ran while one was open for 66% -> 0% of each run, Pallas kernels for 0% -> 0%
where the time goes in v1:
time: 617 us; the launch traced here: 609 us
  Pallas kernels  350 us (57%)
  local copies, waits for them, and re-layouts  107 us (17%)
  matrix products  103 us (17%)
  other arithmetic  47.7 us (8%)
    pallas_call x1, Pallas kernels, scatter_all(): pl.pallas_call(functools.partial(scatter_kernel, sizes, splits), out_shap...  183 us
    pallas_call x1, Pallas kernels, gather_all(): pl.pallas_call(functools.partial(gather_kernel, sizes, splits), out_shape...  167 us
    dot_general x9, matrix products, dot_low(): return jnp.dot(left_side, right_side, preferred_element_type=jnp.float32)  41.5 us
    dot_general x9, matrix products, inner_rows(): lax.dot_general(left_side, right_side, (((0,), (0,)), ((), ())), preferre...  35.3 us
    reshape x8, local copies, waits for them, and re-layouts, unpacked(): array_item[:, i * rows:(i + 1) * rows].reshape(count * rows, width)  32.4 us
    concatenate x8, local copies, waits for them, and re-layouts, spread(): jnp.concatenate([p.astype(low).reshape(count, -1, width) for p in parts],...  30.8 us
    concatenate x2, other arithmetic, spread(): jnp.concatenate([p.astype(low).reshape(count, -1, width) for p in parts],...  19.4 us
    slice x2, local copies, waits for them, and re-layouts, unpacked(): array_item[:, i * rows:(i + 1) * rows].reshape(count * rows, width)  14.9 us

profile of v1, /device:TPU:0, one launch (start us, length us, event | category | flops | bytes accessed | tf_op | source)
XLA Modules:
  0.0 608.7 jit_solution(8141840167005762156)
XLA Ops:
  6.6 167.4 %shard_map.305 = (bf16[4,2,2,272,1088]{4,3,2,1,0:T(8,128)(2,1)}, bf16[4,2,2,272,1088]{4,3,2,1,0:T(8,128)(2,1)}, bf16[4,2,2,272,1088]{4,3,2,1,0:T(8,128)(2,1)}, bf16[4,2,2,12,68]{4,3,2,1,0:T(8,128)(2,1)}) custom-call(bf16[272,1088]{1,0:T(8,128)(2,1)} %get-tuple-element.126.refs_0_, bf16[272,1088]{1,0:T(8,128)(2,1)} %get-tuple-element.127.refs_1_, ...), custom_call_target="tpu_custom_call" | custom-call | tf_op jit(solution)/shard_map/pallas_call | solution.py:197
  175.3 7.4 %fusion.103 = (bf16[16,68,1088]{2,1,0:T(8,128)(2,1)}, bf16[16,68,1088]{2,1,0:T(8,128)(2,1)}, bf16[16,68,1088]{2,1,0:T(8,128)(2,1)S(1)}, bf16[16,68,1088]{2,1,0:T(8,128)(2,1)}) fusion(bf16[16,272,1088]{2,1,0:T(8,128)(2,1)} %bitcast.95), kind=kLoop, calls=%fused_computation.186 | loop fusion | bytes 18939904 | tf_op jit(solution)/shard_map/slice | solution.py:585
  182.7 4.5 reshape.282
  204.2 4.9 fusion.107
  212.9 4.4 reshape.289
  224.4 7.5 %fusion.102 = (bf16[16,68,1088]{2,1,0:T(8,128)(2,1)}, bf16[16,68,1088]{2,1,0:T(8,128)(2,1)}, bf16[16,68,1088]{2,1,0:T(8,128)(2,1)}, bf16[16,68,1088]{2,1,0:T(8,128)(2,1)}) fusion(bf16[16,272,1088]{2,1,0:T(8,128)(2,1)} %bitcast.94), kind=kLoop, calls=%fused_computation.185 | loop fusion | bytes 18939904 | tf_op jit(solution)/shard_map/slice | solution.py:585
  231.9 4.9 reshape.294
  236.8 4.4 multiply_convert_fusion.1
  241.3 4.4 reshape.293
  245.7 4.4 multiply_convert_fusion.2
  250.2 4.4 reshape.292
  254.7 4.4 multiply_convert_fusion.3
  259.2 4.4 reshape.291
  263.6 4.5 multiply_convert_fusion.4
  268.2 9.1 %fusion.6 = bf16[256,1088]{0,1:T(8,128)(2,1)} fusion(f32[256,1088]{0,1:T(8,128)S(1)} %copy-done.5, bf16[4352,1088]{1,0:T(8,128)(2,1)} %bitcast.96, f32[1088]{0:T(1024)S(1)} %add.292, bf16[256,1088]{0,1:T(8,128)(2,1)S(1)} %copy-done.46, bf16[256,1088]{0,1:T(8,128)(2,1)S(1)} %copy-done.48, bf16[256,1088]{0,1:T(8,128)(2,1)} %get-tuple-element.106, ...), kind=kOutput, calls=%fused_computation.36 | convolution fusion | flops 2434056192 | bytes 13373696 | tf_op jit(solution)/shard_map/dot_general | solution.py:485
  334.8 9.7 %pad_maximum_fusion.refs_0_ = bf16[4,2,2,272,1088]{4,3,2,1,0:T(8,128)(2,1)} fusion(bf16[4,2,2,68,1088]{4,3,2,1,0:T(8,128)(2,1)S(1)} %concatenate.45, bf16[4,2,2,68,1088]{4,3,2,1,0:T(8,128)(2,1)} %concatenate.44, bf16[4,2,2,68,1088]{4,3,2,1,0:T(8,128)(2,1)} %concatenate.43, bf16[4,2,2,68,1088]{4,3,2,1,0:T(8,128)(2,1)} %concatenate.42), kind=kLoop, calls=%fused_computation.2 | loop fusion | flops 37879808 | bytes 18939904 | tf_op jit(solution)/shard_map/concatenate | solution.py:653
  352.9 4.5 concatenate.49
  360.8 4.2 concatenate.48
  368.4 4.2 concatenate.47
  372.7 9.7 %pad_maximum_fusion.1.refs_1_ = bf16[4,2,2,272,1088]{4,3,2,1,0:T(8,128)(2,1)} fusion(bf16[4,2,2,68,1088]{4,3,2,1,0:T(8,128)(2,1)S(1)} %concatenate.50, bf16[4,2,2,68,1088]{4,3,2,1,0:T(8,128)(2,1)} %concatenate.49, bf16[4,2,2,68,1088]{4,3,2,1,0:T(8,128)(2,1)} %concatenate.48, bf16[4,2,2,68,1088]{4,3,2,1,0:T(8,128)(2,1)} %concatenate.47), kind=kLoop, calls=%fused_computation.3 | loop fusion | flops 37879808 | bytes 18939904 | tf_op jit(solution)/shard_map/concatenate | solution.py:653
  382.4 9.7 %convolution_convert_fusion = bf16[4352,1088]{0,1:T(8,128)(2,1)} fusion(bf16[256,1088]{0,1:T(8,128)(2,1)S(1)} %copy-done.47, bf16[256,1088]{0,1:T(8,128)(2,1)S(1)} %copy-done.49, bf16[256,1088]{0,1:T(8,128)(2,1)S(1)} %copy-done.50, bf16[256,1088]{0,1:T(8,128)(2,1)S(1)} %copy-done.51, bf16[256,1088]{0,1:T(8,128)(2,1)S(1)} %copy-done.21, ...), kind=kOutput, calls=%fused_computation.1 | convolution fusion | flops 2438791168 | bytes 12256256 | tf_op jit(solution)/shard_map/dot_general | solution.py:489
  392.1 14.0 %copy.49 = bf16[4352,1088]{1,0:T(8,128)(2,1)} copy(bf16[4352,1088]{0,1:T(8,128)(2,1)} %convolution_convert_fusion) | data formatting | bytes 18939904 | tf_op jit(solution)/shard_map/convert_element_type | solution.py:653
  407.6 182.8 %shard_map.306 = (f32[272,1088]{1,0:T(8,128)}, f32[272,1088]{1,0:T(8,128)}, f32[272,1088]{1,0:T(8,128)}, f32[12,1088]{1,0:T(8,128)}) custom-call(bf16[4,2,2,272,1088]{4,3,2,1,0:T(8,128)(2,1)} %pad_maximum_fusion.refs_0_, bf16[4,2,2,272,1088]{4,3,2,1,0:T(8,128)(2,1)} %pad_maximum_fusion.1.refs_1_, bf16[4,2,2,272,1088]{4,3,2,1,0:T(8,128)(2,1)} %bitcast.93, ...), custom_call_target="tpu_custom_call" | custom-call | tf_op jit(solution)/shard_map/pallas_call | solution.py:437
  600.2 4.4 multiply_subtract_fusion.1
  (217 shorter events, 122.8 us)
Async XLA Ops:
  182.7 4.7 copy-start
  187.8 4.1 copy-start.40
  263.6 4.6 copy-start.5
  263.6 4.6 copy-start.46
  263.6 4.6 copy-start.48
  263.6 13.7 %slice-start = ((s8[10027008]{0:T(1024)(128)(4,1)}), s8[4194304]{0:T(1024)(128)(4,1)S(1)}, s32[]{:S(2)}) async-start(s8[10027008]{0:T(1024)(128)(4,1)} %bitcast.97), calls=%async_computation | async-start | bytes 8388608
  268.2 9.1 %slice-start.1 = ((s8[10027008]{0:T(1024)(128)(4,1)}), s8[4194304]{0:T(1024)(128)(4,1)S(1)}, s32[]{:S(2)}) async-start(s8[10027008]{0:T(1024)(128)(4,1)} %bitcast.97), calls=%async_computation.1 | async-start | bytes 8388608
  268.2 9.1 %slice-start.2 = ((s8[10027008]{0:T(1024)(128)(4,1)}), s8[1638400]{0:T(1024)(128)(4,1)S(1)}, s32[]{:S(2)}) async-start(s8[10027008]{0:T(1024)(128)(4,1)} %bitcast.97), calls=%async_computation.2 | async-start | bytes 3276800
  290.4 3.9 slice-start.3
  334.8 9.7 %copy-start.3 = (bf16[256,1088]{0,1:T(8,128)(2,1)S(1)}, bf16[256,1088]{0,1:T(8,128)(2,1)}, u32[]{:S(2)}) copy-start(bf16[256,1088]{0,1:T(8,128)(2,1)} %add_convert_fusion.1) | copy-start | bytes 1671172
  334.8 9.7 %copy-start.32 = (bf16[256,1088]{0,1:T(8,128)(2,1)S(1)}, bf16[256,1088]{0,1:T(8,128)(2,1)}, u32[]{:S(2)}) copy-start(bf16[256,1088]{0,1:T(8,128)(2,1)} %copy-done.31) | copy-start | bytes 1671172
  372.7 9.7 %copy-start.21 = (bf16[256,1088]{0,1:T(8,128)(2,1)S(1)}, bf16[256,1088]{0,1:T(8,128)(2,1)}, u32[]{:S(2)}) copy-start(bf16[256,1088]{0,1:T(8,128)(2,1)} %param.19) | copy-start | bytes 1671172
  372.7 9.7 %copy-start.47 = (bf16[256,1088]{0,1:T(8,128)(2,1)S(1)}, bf16[256,1088]{0,1:T(8,128)(2,1)}, u32[]{:S(2)}) copy-start(bf16[256,1088]{0,1:T(8,128)(2,1)} %get-tuple-element.102) | copy-start | bytes 1671172
  372.7 9.7 %copy-start.49 = (bf16[256,1088]{0,1:T(8,128)(2,1)S(1)}, bf16[256,1088]{0,1:T(8,128)(2,1)}, u32[]{:S(2)}) copy-start(bf16[256,1088]{0,1:T(8,128)(2,1)} %get-tuple-element.104) | copy-start | bytes 1671172
  372.7 9.7 %copy-start.50 = (bf16[256,1088]{0,1:T(8,128)(2,1)S(1)}, bf16[256,1088]{0,1:T(8,128)(2,1)}, u32[]{:S(2)}) copy-start(bf16[256,1088]{0,1:T(8,128)(2,1)} %get-tuple-element.106) | copy-start | bytes 1671172
  372.7 9.7 %copy-start.51 = (bf16[256,1088]{0,1:T(8,128)(2,1)S(1)}, bf16[256,1088]{0,1:T(8,128)(2,1)}, u32[]{:S(2)}) copy-start(bf16[256,1088]{0,1:T(8,128)(2,1)} %get-tuple-element.108) | copy-start | bytes 1671172
  407.6 182.8 %copy-start.23 = (f32[68,1088]{1,0:T(8,128)S(1)}, f32[68,1088]{1,0:T(8,128)}, u32[]{:S(2)}) copy-start(f32[68,1088]{1,0:T(8,128)} %param.24) | copy-start | bytes 887812
  407.6 182.8 %copy-start.34 = (f32[68,1088]{1,0:T(8,128)S(1)}, f32[68,1088]{1,0:T(8,128)}, u32[]{:S(2)}) copy-start(f32[68,1088]{1,0:T(8,128)} %param.25) | copy-start | bytes 887812
  407.6 182.8 %copy-start.35 = (f32[68,1088]{1,0:T(8,128)S(1)}, f32[68,1088]{1,0:T(8,128)}, u32[]{:S(2)}) copy-start(f32[68,1088]{1,0:T(8,128)} %param.26) | copy-start | bytes 887812
  594.1 3.7 copy-start.22
  600.1 4.4 copy-start.10
  600.1 4.4 copy-start.24
  600.1 4.4 copy-start.25
  600.1 4.4 copy-start.26
  (33 other events, 53.6 us)

commit v2 on v1

--- a/solution.py
+++ b/solution.py
@@ -34,6 +34,20 @@
     tiles = rows // 16
     first = 16 * ((tiles + 1) // 2 if not flip else tiles // 2)
     return ((0, first), (first, rows - first))
+
+
+def pieces_of(rows, arrays):
+    parts = 2 if rows >= 256 else 1
+    found = []
+    for array in range(arrays):
+        spans = row_split(rows, array % 2 == 1)
+        for part in range(parts):
+            both = []
+            for start, height in spans:
+                first = height if parts == 1 else 16 * ((height // 16 + 1) // 2)
+                both.append((start, first) if part == 0 else (start + first, height - first))
+            found.append((array, tuple(both)))
+    return tuple(array for array, _ in found), tuple(both for _, both in found)
 
 
 def place(sizes):
@@ -66,10 +80,12 @@
     )
 
 
-def gather_kernel(sizes, splits, *refs):
+def gather_kernel(sizes, homes, splits, *refs):
+    count = homes[-1] + 1
     arrays = len(splits)
-    ins, outs = refs[: arrays + 1], refs[arrays + 1 : 2 * arrays + 2]
-    (local_sem, zs_sem, zr_sem, as_sem, ar_sem, bs_sem, br_sem, ps_sem, pr_sem) = refs[2 * arrays + 2 :]
+    homes = homes + (count,)
+    ins, outs = refs[: count + 1], refs[count + 1 : 2 * count + 2]
+    (local_sem, zs_sem, zr_sem, as_sem, ar_sem, bs_sem, br_sem, ps_sem, pr_sem) = refs[2 * count + 2 :]
     size_z, side, _ = sizes
     core, z, y, x = place(sizes)
     greet(sizes, core, z, y, x)
@@ -90,9 +106,9 @@
 
         def line(k, yx):
             if k == arrays:
-                return outs[k].at[:, yx[0], yx[1]]
+                return outs[homes[k]].at[:, yx[0], yx[1]]
             start, rows = splits[k][c]
-            return outs[k].at[:, yx[0], yx[1], pl.ds(start, rows), :]
+            return outs[homes[k]].at[:, yx[0], yx[1], pl.ds(start, rows), :]
 
         def go(copy):
             copy.start()
@@ -115,9 +131,9 @@
 
         def block(k):
             if k == arrays:
-                return ins[k], outs[k].at[z, y, x]
+                return ins[homes[k]], outs[homes[k]].at[z, y, x]
             start, rows = splits[k][c]
-            return ins[k].at[pl.ds(start, rows), :], outs[k].at[z, y, x, pl.ds(start, rows), :]
+            return ins[homes[k]].at[pl.ds(start, rows), :], outs[homes[k]].at[z, y, x, pl.ds(start, rows), :]
 
         def z_copy(k, d):
             src, dst = block(k)
@@ -131,15 +147,22 @@
             return pltpu.make_async_copy(src, dst, local_sem.at[k])
 
         order = [arrays] + list(range(arrays))
+
+        def begin(k):
+            for d in range(1, size_z):
+                go(z_copy(k, d))
+
         for k in order:
             own_copy(k).start()
-            for d in range(1, size_z):
-                go(z_copy(k, d))
+        for k in order[:3]:
+            begin(k)
 
         def stage_one(k):
             own_copy(k).wait()
             for d in range(1, size_z):
                 z_copy(k, d).wait_recv()
+            if k < arrays and k + 2 < arrays:
+                begin(k + 2)
             for d in range(1, side):
                 go(second_copy(k, d))
             for d in range(1, side):
@@ -176,7 +199,7 @@
                     a = lax.rem(theirs[0] + side - d2, side)
                     b = lax.rem(theirs[1] + side - d3, side)
                     yx = (a, b) if c == 0 else (b, a)
-                    ref = outs[k].at[:, yx[0], yx[1], pl.ds(start, rows), :]
+                    ref = outs[homes[k]].at[:, yx[0], yx[1], pl.ds(start, rows), :]
                     remote(
                         ref, ref, ps_sem.at[k, d2, d3], pr_sem.at[k, d2, d3],
                         (1 - core, chip_id(sizes, z, y, x)),
@@ -189,16 +212,16 @@
 
 
 def gather_all(sizes, shards, vector_shard):
-    arrays = len(shards)
     size_z, side, _ = sizes
-    splits = tuple(row_split(s.shape[0], k % 2 == 1) for k, s in enumerate(shards))
+    homes, splits = pieces_of(shards[0].shape[0], len(shards))
+    arrays = len(splits)
     everything = tuple(shards) + (vector_shard,)
     dma = pltpu.SemaphoreType.DMA
     return pl.pallas_call(
-        functools.partial(gather_kernel, sizes, splits),
+        functools.partial(gather_kernel, sizes, homes, splits),
         out_shape=[jax.ShapeDtypeStruct(sizes + s.shape, s.dtype) for s in everything],
-        in_specs=[pl.BlockSpec(memory_space=pl.ANY)] * (arrays + 1),
-        out_specs=[pl.BlockSpec(memory_space=pl.ANY)] * (arrays + 1),
+        in_specs=[pl.BlockSpec(memory_space=pl.ANY)] * len(everything),
+        out_specs=[pl.BlockSpec(memory_space=pl.ANY)] * len(everything),
         scratch_shapes=[
             dma((arrays + 1,)),
             dma((arrays + 1, size_z)), dma((arrays + 1, size_z)),
@@ -229,13 +252,14 @@
     lax.fori_loop(0, steps, body, 0)
 
 
-def scatter_kernel(sizes, splits, *refs):
+def scatter_kernel(sizes, homes, splits, *refs):
+    given = homes[-1] + 1
     arrays = len(splits)
-    ins, vec_in = refs[:arrays], refs[arrays]
-    outs, vec_out = refs[arrays + 1 : 2 * arrays + 1], refs[2 * arrays + 1]
+    ins, vec_in = refs[:given], refs[given]
+    outs, vec_out = refs[given + 1 : 2 * given + 1], refs[2 * given + 1]
     (own, part, second, third, fourth, result, vec_slots,
      load_sem, store_sem, as_sem, ar_sem, bs_sem, br_sem, cs_sem, cr_sem, ds_sem, dr_sem,
-     es_sem, er_sem, vs_sem, vr_sem, credit) = refs[2 * arrays + 2 :]
+     es_sem, er_sem, vs_sem, vr_sem, credit) = refs[2 * given + 2 :]
     size_z, side, _ = sizes
     core, z, y, x = place(sizes)
     greet(sizes, core, z, y, x)
@@ -257,12 +281,12 @@
 
         def load(k):
             return pltpu.make_async_copy(
-                ins[k].at[:, :, :, rows_of(k, c), :], own.at[k, :, :, :, height(k), :], load_sem.at[k]
+                ins[homes[k]].at[:, :, :, rows_of(k, c), :], own.at[k, :, :, :, height(k), :], load_sem.at[k]
             )
 
         def swap(k):
             return remote(
-                ins[k].at[:, :, :, rows_of(k, 1 - c), :],
+                ins[homes[k]].at[:, :, :, rows_of(k, 1 - c), :],
                 part.at[k % 2, :, :, :, height(k, 1 - c), :],
                 as_sem.at[k], ar_sem.at[k], partner,
             )
@@ -343,12 +367,12 @@
 
         def finish(k):
             return remote(
-                result.at[k, height(k), :], outs[k].at[rows_of(k, c), :], es_sem.at[k], er_sem.at[k], partner
+                result.at[k, height(k), :], outs[homes[k]].at[rows_of(k, c), :], es_sem.at[k], er_sem.at[k], partner
             )
 
         def store(k):
             return pltpu.make_async_copy(
-                result.at[k, height(k), :], outs[k].at[rows_of(k, c), :], store_sem.at[k]
+                result.at[k, height(k), :], outs[homes[k]].at[rows_of(k, c), :], store_sem.at[k]
             )
 
         def stage_d(k):
@@ -415,7 +439,7 @@
         for k in range(arrays):
             store(k).wait()
             start, rows = splits[k][1 - c]
-            ref = outs[k].at[pl.ds(start, rows), :]
+            ref = outs[homes[k]].at[pl.ds(start, rows), :]
             remote(ref, ref, es_sem.at[k], er_sem.at[k], partner).wait_recv()
         for copy in sends:
             copy.wait_send()
@@ -425,22 +449,22 @@
 
 
 def scatter_all(sizes, terms, vector_term):
-    arrays = len(terms)
     size_z, side, _ = sizes
     rows, width = terms[0].shape[-2:]
-    splits = tuple(row_split(rows, k % 2 == 1) for k in range(arrays))
+    homes, splits = pieces_of(rows, len(terms))
+    arrays = len(splits)
     most = max(part[1] for split in splits for part in split)
     dma = pltpu.SemaphoreType.DMA
     low = jnp.bfloat16
     pair = [dma((arrays,)), dma((arrays,))]
     sides = [dma((arrays, side)), dma((arrays, side))]
     return pl.pallas_call(
-        functools.partial(scatter_kernel, sizes, splits),
+        functools.partial(scatter_kernel, sizes, homes, splits),
         out_shape=[jax.ShapeDtypeStruct((rows, width), jnp.float32) for _ in terms]
         + [jax.ShapeDtypeStruct(vector_term.shape, jnp.float32)],
-        in_specs=[pl.BlockSpec(memory_space=pl.ANY)] * arrays
+        in_specs=[pl.BlockSpec(memory_space=pl.ANY)] * len(terms)
         + [pl.BlockSpec(memory_space=pltpu.VMEM)],
-        out_specs=[pl.BlockSpec(memory_space=pl.ANY)] * arrays
+        out_specs=[pl.BlockSpec(memory_space=pl.ANY)] * len(terms)
         + [pl.BlockSpec(memory_space=pltpu.VMEM)],
         scratch_shapes=[
             pltpu.VMEM((arrays,) + sizes + (most, width), low),

time: 617 us -> 585 us (0.948)
  Pallas kernels: 350 us -> 319 us
    pallas_call x2, Pallas kernels: 350 us -> 319 us  [the longest x1 168 us: scatter_all(): pl.pallas_call(functools.partial(scatter_kernel, sizes, homes, splits), o...]
where the time goes in v2:
time: 585 us; the launch traced here: 577 us
  Pallas kernels  319 us (55%)
  local copies, waits for them, and re-layouts  107 us (18%)
  matrix products  103 us (18%)
  other arithmetic  47.7 us (8%)
    pallas_call x1, Pallas kernels, scatter_all(): pl.pallas_call(functools.partial(scatter_kernel, sizes, homes, splits), o...  168 us
    pallas_call x1, Pallas kernels, gather_all(): pl.pallas_call(functools.partial(gather_kernel, sizes, homes, splits), ou...  151 us
    dot_general x9, matrix products, dot_low(): return jnp.dot(left_side, right_side, preferred_element_type=jnp.float32)  41.5 us
    dot_general x9, matrix products, inner_rows(): lax.dot_general(left_side, right_side, (((0,), (0,)), ((), ())), preferre...  35.3 us
    reshape x8, local copies, waits for them, and re-layouts, unpacked(): array_item[:, i * rows:(i + 1) * rows].reshape(count * rows, width)  32.4 us
    concatenate x8, local copies, waits for them, and re-layouts, spread(): jnp.concatenate([p.astype(low).reshape(count, -1, width) for p in parts],...  30.8 us
    concatenate x2, other arithmetic, spread(): jnp.concatenate([p.astype(low).reshape(count, -1, width) for p in parts],...  19.4 us
    slice x2, local copies, waits for them, and re-layouts, unpacked(): array_item[:, i * rows:(i + 1) * rows].reshape(count * rows, width)  14.9 us

profile of v2, /device:TPU:0, one launch (start us, length us, event | category | flops | bytes accessed | tf_op | source)
XLA Modules:
  0.0 577.3 jit_solution(8449005587418900478)
XLA Ops:
  6.6 150.9 %shard_map.305 = (bf16[4,2,2,272,1088]{4,3,2,1,0:T(8,128)(2,1)}, bf16[4,2,2,272,1088]{4,3,2,1,0:T(8,128)(2,1)}, bf16[4,2,2,272,1088]{4,3,2,1,0:T(8,128)(2,1)}, bf16[4,2,2,12,68]{4,3,2,1,0:T(8,128)(2,1)}) custom-call(bf16[272,1088]{1,0:T(8,128)(2,1)} %get-tuple-element.126.refs_0_, bf16[272,1088]{1,0:T(8,128)(2,1)} %get-tuple-element.127.refs_1_, ...), custom_call_target="tpu_custom_call" | custom-call | tf_op jit(solution)/shard_map/pallas_call | solution.py:220
  158.7 7.4 %fusion.103 = (bf16[16,68,1088]{2,1,0:T(8,128)(2,1)}, bf16[16,68,1088]{2,1,0:T(8,128)(2,1)}, bf16[16,68,1088]{2,1,0:T(8,128)(2,1)S(1)}, bf16[16,68,1088]{2,1,0:T(8,128)(2,1)}) fusion(bf16[16,272,1088]{2,1,0:T(8,128)(2,1)} %bitcast.95), kind=kLoop, calls=%fused_computation.186 | loop fusion | bytes 18939904 | tf_op jit(solution)/shard_map/slice | solution.py:609
  166.1 4.5 reshape.282
  187.7 4.9 fusion.107
  196.3 4.4 reshape.289
  207.9 7.5 %fusion.102 = (bf16[16,68,1088]{2,1,0:T(8,128)(2,1)}, bf16[16,68,1088]{2,1,0:T(8,128)(2,1)}, bf16[16,68,1088]{2,1,0:T(8,128)(2,1)}, bf16[16,68,1088]{2,1,0:T(8,128)(2,1)}) fusion(bf16[16,272,1088]{2,1,0:T(8,128)(2,1)} %bitcast.94), kind=kLoop, calls=%fused_computation.185 | loop fusion | bytes 18939904 | tf_op jit(solution)/shard_map/slice | solution.py:609
  215.4 4.9 reshape.294
  220.2 4.4 multiply_convert_fusion.1
  224.8 4.4 reshape.293
  229.2 4.4 multiply_convert_fusion.2
  233.7 4.4 reshape.292
  238.1 4.4 multiply_convert_fusion.3
  242.6 4.4 reshape.291
  247.1 4.5 multiply_convert_fusion.4
  251.6 9.1 %fusion.6 = bf16[256,1088]{0,1:T(8,128)(2,1)} fusion(f32[256,1088]{0,1:T(8,128)S(1)} %copy-done.5, bf16[4352,1088]{1,0:T(8,128)(2,1)} %bitcast.96, f32[1088]{0:T(1024)S(1)} %add.292, bf16[256,1088]{0,1:T(8,128)(2,1)S(1)} %copy-done.46, bf16[256,1088]{0,1:T(8,128)(2,1)S(1)} %copy-done.48, bf16[256,1088]{0,1:T(8,128)(2,1)} %get-tuple-element.106, ...), kind=kOutput, calls=%fused_computation.36 | convolution fusion | flops 2434056192 | bytes 13373696 | tf_op jit(solution)/shard_map/dot_general | solution.py:509
  318.3 9.7 %pad_maximum_fusion.refs_0_ = bf16[4,2,2,272,1088]{4,3,2,1,0:T(8,128)(2,1)} fusion(bf16[4,2,2,68,1088]{4,3,2,1,0:T(8,128)(2,1)S(1)} %concatenate.45, bf16[4,2,2,68,1088]{4,3,2,1,0:T(8,128)(2,1)} %concatenate.44, bf16[4,2,2,68,1088]{4,3,2,1,0:T(8,128)(2,1)} %concatenate.43, bf16[4,2,2,68,1088]{4,3,2,1,0:T(8,128)(2,1)} %concatenate.42), kind=kLoop, calls=%fused_computation.2 | loop fusion | flops 37879808 | bytes 18939904 | tf_op jit(solution)/shard_map/concatenate | solution.py:677
  336.3 4.5 concatenate.49
  344.3 4.2 concatenate.48
  351.9 4.2 concatenate.47
  356.1 9.7 %pad_maximum_fusion.1.refs_1_ = bf16[4,2,2,272,1088]{4,3,2,1,0:T(8,128)(2,1)} fusion(bf16[4,2,2,68,1088]{4,3,2,1,0:T(8,128)(2,1)S(1)} %concatenate.50, bf16[4,2,2,68,1088]{4,3,2,1,0:T(8,128)(2,1)} %concatenate.49, bf16[4,2,2,68,1088]{4,3,2,1,0:T(8,128)(2,1)} %concatenate.48, bf16[4,2,2,68,1088]{4,3,2,1,0:T(8,128)(2,1)} %concatenate.47), kind=kLoop, calls=%fused_computation.3 | loop fusion | flops 37879808 | bytes 18939904 | tf_op jit(solution)/shard_map/concatenate | solution.py:677
  365.9 9.7 %convolution_convert_fusion = bf16[4352,1088]{0,1:T(8,128)(2,1)} fusion(bf16[256,1088]{0,1:T(8,128)(2,1)S(1)} %copy-done.47, bf16[256,1088]{0,1:T(8,128)(2,1)S(1)} %copy-done.49, bf16[256,1088]{0,1:T(8,128)(2,1)S(1)} %copy-done.50, bf16[256,1088]{0,1:T(8,128)(2,1)S(1)} %copy-done.51, bf16[256,1088]{0,1:T(8,128)(2,1)S(1)} %copy-done.21, ...), kind=kOutput, calls=%fused_computation.1 | convolution fusion | flops 2438791168 | bytes 12256256 | tf_op jit(solution)/shard_map/dot_general | solution.py:513
  375.5 14.0 %copy.49 = bf16[4352,1088]{1,0:T(8,128)(2,1)} copy(bf16[4352,1088]{0,1:T(8,128)(2,1)} %convolution_convert_fusion) | data formatting | bytes 18939904 | tf_op jit(solution)/shard_map/convert_element_type | solution.py:677
  391.1 167.9 %shard_map.306 = (f32[272,1088]{1,0:T(8,128)}, f32[272,1088]{1,0:T(8,128)}, f32[272,1088]{1,0:T(8,128)}, f32[12,1088]{1,0:T(8,128)}) custom-call(bf16[4,2,2,272,1088]{4,3,2,1,0:T(8,128)(2,1)} %pad_maximum_fusion.refs_0_, bf16[4,2,2,272,1088]{4,3,2,1,0:T(8,128)(2,1)} %pad_maximum_fusion.1.refs_1_, bf16[4,2,2,272,1088]{4,3,2,1,0:T(8,128)(2,1)} %bitcast.93, ...), custom_call_target="tpu_custom_call" | custom-call | tf_op jit(solution)/shard_map/pallas_call | solution.py:461
  568.7 4.4 multiply_subtract_fusion.1
  (217 shorter events, 122.8 us)
Async XLA Ops:
  166.1 4.7 copy-start
  171.3 4.1 copy-start.40
  247.1 4.6 copy-start.5
  247.1 4.6 copy-start.46
  247.1 4.6 copy-start.48
  247.1 13.7 %slice-start = ((s8[10027008]{0:T(1024)(128)(4,1)}), s8[4194304]{0:T(1024)(128)(4,1)S(1)}, s32[]{:S(2)}) async-start(s8[10027008]{0:T(1024)(128)(4,1)} %bitcast.97), calls=%async_computation | async-start | bytes 8388608
  251.6 9.1 %slice-start.1 = ((s8[10027008]{0:T(1024)(128)(4,1)}), s8[4194304]{0:T(1024)(128)(4,1)S(1)}, s32[]{:S(2)}) async-start(s8[10027008]{0:T(1024)(128)(4,1)} %bitcast.97), calls=%async_computation.1 | async-start | bytes 8388608
  251.6 9.1 %slice-start.2 = ((s8[10027008]{0:T(1024)(128)(4,1)}), s8[1638400]{0:T(1024)(128)(4,1)S(1)}, s32[]{:S(2)}) async-start(s8[10027008]{0:T(1024)(128)(4,1)} %bitcast.97), calls=%async_computation.2 | async-start | bytes 3276800
  273.8 3.9 slice-start.3
  318.2 9.7 %copy-start.3 = (bf16[256,1088]{0,1:T(8,128)(2,1)S(1)}, bf16[256,1088]{0,1:T(8,128)(2,1)}, u32[]{:S(2)}) copy-start(bf16[256,1088]{0,1:T(8,128)(2,1)} %add_convert_fusion.1) | copy-start | bytes 1671172
  318.2 9.7 %copy-start.32 = (bf16[256,1088]{0,1:T(8,128)(2,1)S(1)}, bf16[256,1088]{0,1:T(8,128)(2,1)}, u32[]{:S(2)}) copy-start(bf16[256,1088]{0,1:T(8,128)(2,1)} %copy-done.31) | copy-start | bytes 1671172
  356.1 9.7 %copy-start.21 = (bf16[256,1088]{0,1:T(8,128)(2,1)S(1)}, bf16[256,1088]{0,1:T(8,128)(2,1)}, u32[]{:S(2)}) copy-start(bf16[256,1088]{0,1:T(8,128)(2,1)} %param.19) | copy-start | bytes 1671172
  356.1 9.7 %copy-start.47 = (bf16[256,1088]{0,1:T(8,128)(2,1)S(1)}, bf16[256,1088]{0,1:T(8,128)(2,1)}, u32[]{:S(2)}) copy-start(bf16[256,1088]{0,1:T(8,128)(2,1)} %get-tuple-element.102) | copy-start | bytes 1671172
  356.1 9.7 %copy-start.49 = (bf16[256,1088]{0,1:T(8,128)(2,1)S(1)}, bf16[256,1088]{0,1:T(8,128)(2,1)}, u32[]{:S(2)}) copy-start(bf16[256,1088]{0,1:T(8,128)(2,1)} %get-tuple-element.104) | copy-start | bytes 1671172
  356.1 9.7 %copy-start.50 = (bf16[256,1088]{0,1:T(8,128)(2,1)S(1)}, bf16[256,1088]{0,1:T(8,128)(2,1)}, u32[]{:S(2)}) copy-start(bf16[256,1088]{0,1:T(8,128)(2,1)} %get-tuple-element.106) | copy-start | bytes 1671172
  356.1 9.7 %copy-start.51 = (bf16[256,1088]{0,1:T(8,128)(2,1)S(1)}, bf16[256,1088]{0,1:T(8,128)(2,1)}, u32[]{:S(2)}) copy-start(bf16[256,1088]{0,1:T(8,128)(2,1)} %get-tuple-element.108) | copy-start | bytes 1671172
  391.1 167.9 %copy-start.23 = (f32[68,1088]{1,0:T(8,128)S(1)}, f32[68,1088]{1,0:T(8,128)}, u32[]{:S(2)}) copy-start(f32[68,1088]{1,0:T(8,128)} %param.24) | copy-start | bytes 887812
  391.1 167.9 %copy-start.34 = (f32[68,1088]{1,0:T(8,128)S(1)}, f32[68,1088]{1,0:T(8,128)}, u32[]{:S(2)}) copy-start(f32[68,1088]{1,0:T(8,128)} %param.25) | copy-start | bytes 887812
  391.1 167.9 %copy-start.35 = (f32[68,1088]{1,0:T(8,128)S(1)}, f32[68,1088]{1,0:T(8,128)}, u32[]{:S(2)}) copy-start(f32[68,1088]{1,0:T(8,128)} %param.26) | copy-start | bytes 887812
  562.7 3.7 copy-start.22
  568.7 4.4 copy-start.10
  568.7 4.4 copy-start.24
  568.7 4.4 copy-start.25
  568.7 4.4 copy-start.26
  (33 other events, 53.6 us)
